TPU v7x, 32 devices: a whole 2x2x4 slice. The times are simulated.
32 devices in a mesh: tile: 8 (over z, y), head: 4 (over x, core).
Axes of the slice: x: 2, y: 2, z: 4, core: 2. Of those that a mesh axis runs over, the one named last changes fastest.
Arguments:
- latents: bfloat16 [7200, 5120], P('tile'), may hold values from -1000 to 1000
- query_weight: bfloat16 [5120, 2560], P('tile', 'head'), may hold values from -1.5 to 1.5
- mod_shift: float32 [5120], replicated, may hold values from -3 to 3
- mod_scale: float32 [5120], replicated, may hold values from -3 to 3
- query_gain: float32 [2560], P('head'), may hold values from 0.5 to 2
- cache_blocks: bfloat16 [7200, 2, 2560], P('tile', None, 'head'), may hold values from -640 to 640
- block_counts: int32 [8], replicated, may hold values from 1 to 900, 5400 in all
- group_index: int32 [1], replicated, may hold values from 1 to 20
Outputs:
- attended: bfloat16 [7200, 2560], P('tile', 'head')
Inputs may be any that keep to these rules, and one draw needn't show every extreme that they name: `block_counts`: entry t counts the valid cached tokens of tile t; they are its first ones; the largest entry is exactly 900.
All inputs are finite; a program needn't handle non-finite values.
Results may differ from a plain program's by a relative error of at most 0.008.
The roundings to bfloat16 on the way count: a program that leaves them out, or rounds other values in their place, can miss the bound.
Values may be sent and summed in bfloat16 or wider, within the bound.
A program may use at most 128 MiB of HBM per device.

v0:
```python
import math

import jax
import jax.numpy as jnp
import numpy as np
from jax import lax
from jax.sharding import PartitionSpec as P

D = 5120
HEADS = 20
HD = 128
FRAMES = 3
WINDOW = 1
GH = 45
GW = 80


norm_eps = 1e-06


def from_partner(value, axis, stride):
    mask = 2**stride
    pairs = [(source, source ^ mask) for source in range(lax.axis_size(axis))]
    return lax.ppermute(value, axis, pairs)


def rotary_tables(place_index, group_value, token_count, head_dim):
    local = place_index * token_count + jnp.arange(token_count, dtype=jnp.int32)
    frame_pos = local // (GH * GW)
    row_pos = local // GW % GH
    col_pos = local % GW
    time_pos = (group_value * FRAMES + frame_pos).astype(jnp.float32)
    height_pos = row_pos.astype(jnp.float32)
    width_pos = col_pos.astype(jnp.float32)
    half_dim = head_dim // 2
    space_pairs = head_dim // 6
    time_pairs = half_dim - 2 * space_pairs
    pair_index = jnp.arange(half_dim, dtype=jnp.int32)
    in_time = pair_index < time_pairs
    in_height = pair_index < time_pairs + space_pairs
    offset = jnp.where(
        in_time,
        pair_index,
        jnp.where(in_height, pair_index - time_pairs, pair_index - time_pairs - space_pairs),
    )
    extent = jnp.where(in_time, time_pairs, space_pairs)
    theta = jnp.exp(-math.log(10000.0) * offset.astype(jnp.float32) / extent.astype(jnp.float32))
    position = jnp.where(
        in_time[None, :],
        time_pos[:, None],
        jnp.where(in_height[None, :], height_pos[:, None], width_pos[:, None]),
    )
    angle = position * theta[None, :]
    return (jnp.cos(angle), jnp.sin(angle))


def rotate_pairs(scaled, cos_table, sin_table):
    token_count, head_count, head_dim = scaled.shape
    paired = scaled.reshape(token_count, head_count, head_dim // 2, 2)
    first_part = paired[..., 0]
    second_part = paired[..., 1]
    cos_wide = cos_table[:, None, :]
    sin_wide = sin_table[:, None, :]
    turned = jnp.stack(
        [
            first_part * cos_wide - second_part * sin_wide,
            first_part * sin_wide + second_part * cos_wide,
        ],
        axis=-1,
    )
    return turned.reshape(token_count, head_count, head_dim)


def per_device(
    latents, query_weight, mod_shift, mod_scale, query_gain, cache_blocks, block_counts, group_index
):
    token_count = latents.shape[0]
    width_here = query_weight.shape[1]
    heads_here = width_here // HD
    widened = latents.astype(jnp.float32)
    row_mean = jnp.sum(widened, axis=1, keepdims=True) / D
    row_var = jnp.sum(widened * widened, axis=1, keepdims=True) / D - row_mean * row_mean
    normed = (
        (widened - row_mean) * lax.rsqrt(row_var + norm_eps) * (1.0 + mod_scale) + mod_shift
    ).astype(jnp.bfloat16)
    queries = jnp.dot(
        normed,
        lax.all_gather(query_weight, "tile", axis=0, tiled=True),
        preferred_element_type=jnp.float32,
    )
    squares = lax.psum(jnp.sum(queries * queries, axis=1), "head")
    scaled = queries * lax.rsqrt(squares[:, None] / (HEADS * HD) + norm_eps) * query_gain
    clip_span = WINDOW * GH * GW // token_count
    tile_index = lax.axis_index("tile")
    place_index = tile_index % clip_span
    cos_table, sin_table = rotary_tables(place_index, group_index[0], token_count, HD)
    rotated = rotate_pairs(
        scaled.reshape(token_count, heads_here, HD), cos_table, sin_table
    ).astype(jnp.bfloat16)
    rotated_flat = rotated.reshape(token_count, width_here)
    bit_total = clip_span.bit_length() - 1
    bit_sequence = list(range(bit_total))
    cache_rows = cache_blocks
    slot_order = np.zeros(1, np.int32)
    for bit_number in bit_sequence:
        partner = from_partner(cache_rows, "tile", bit_number)
        mine_high = tile_index >> bit_number & 1 == 1
        lower_rows = jnp.where(mine_high, partner, cache_rows)
        upper_rows = jnp.where(mine_high, cache_rows, partner)
        cache_rows = jnp.concatenate([lower_rows, upper_rows], axis=0)
        slot_order = np.concatenate([slot_order, slot_order + (1 << bit_number)])
    clip_base = tile_index - place_index
    counts_here = lax.dynamic_slice_in_dim(block_counts, clip_base, clip_span)
    order_table = jnp.asarray(slot_order, jnp.int32)
    span_numbers = jnp.arange(clip_span, dtype=jnp.int32)
    counts_ordered = jnp.sum(
        jnp.where(span_numbers[None, :] == order_table[:, None], counts_here[None, :], 0), axis=1
    )
    valid_mask = (
        jnp.arange(token_count, dtype=jnp.int32)[None, :] < counts_ordered[:, None]
    ).reshape(-1)
    keys_all = cache_rows[:, 0, :]
    values_all = cache_rows[:, 1, :]
    score_scale = 1.0 / math.sqrt(HD)

    def one_head(head_number):
        first_col = head_number * HD
        query_part = lax.dynamic_slice_in_dim(rotated_flat, first_col, HD, 1)
        key_part = lax.dynamic_slice_in_dim(keys_all, first_col, HD, 1)
        value_part = lax.dynamic_slice_in_dim(values_all, first_col, HD, 1)
        scores = (
            lax.dot_general(
                query_part, key_part, (((1,), (1,)), ((), ())), preferred_element_type=jnp.float32
            )
            * score_scale
        )
        masked = jnp.where(valid_mask[None, :], scores, -1e30)
        top_score = jnp.max(masked, axis=1, keepdims=True)
        weights = jnp.where(valid_mask[None, :], jnp.exp(masked - top_score), 0.0)
        totals = jnp.sum(weights, axis=1, keepdims=True)
        rounded = weights.astype(jnp.bfloat16)
        mixed = jnp.dot(rounded, value_part, preferred_element_type=jnp.float32)
        return (mixed / totals).astype(jnp.bfloat16)

    per_head = lax.map(one_head, jnp.arange(heads_here, dtype=jnp.int32))
    return jnp.transpose(per_head, (1, 0, 2)).reshape(token_count, width_here)


def solution(mesh):
    in_specs = (
        P("tile", None),
        P("tile", "head"),
        P(),
        P(),
        P("head"),
        P("tile", None, "head"),
        P(),
        P(),
    )
    out_specs = P("tile", "head")
    return jax.shard_map(
        per_device, mesh=mesh, in_specs=in_specs, out_specs=out_specs, check_vma=False
    )
```

profile of v0, /device:TPU:1, one launch (start us, length us, event | category | flops | bytes accessed | tf_op | source)
XLA Modules:
  0.0 341.9 jit_solution(11938905609938011056)
XLA Ops:
  6.5 0.7 all-gather.2.cloned.1.call-update
  7.3 2.1 collective-permute-start
  9.4 65.7 %collective-permute-done = bf16[900,2,640]{2,1,0:T(2,128)(2,1)} collective-permute-done((bf16[900,2,640]{2,1,0:T(2,128)(2,1)}, bf16[900,2,640]{2,1,0:T(2,128)(2,1)}, u32[]{:S(2)}, u32[]{:S(2)}) %collective-permute-start) | collective-permute-done | bytes 2304032 | tf_op jit(solution)/shard_map/ppermute | solution.py:24
  75.1 3.2 broadcast_select_fusion.3
  78.3 2.9 pad_maximum_fusion.1
  81.3 1.2 collective-permute-start.1
  83.2 0.1 select_reduce_fusion
  83.4 6.6 %convert_reduce_fusion = (f32[900]{0:T(1024)S(1)}, f32[900]{0:T(1024)S(1)}) fusion(bf16[900,5120]{1,0:T(8,128)(2,1)} %param.11), kind=kLoop, calls=%fused_computation.24 | loop fusion | flops 18430200 | bytes 9223200 | tf_op jit(solution)/shard_map/reduce_sum | solution.py:81
  90.0 1.0 fusion.44
  91.1 120.5 %collective-permute-done.1 = bf16[1800,2,640]{2,0,1:T(8,128)(2,1)} collective-permute-done((bf16[1800,2,640]{2,0,1:T(8,128)(2,1)}, bf16[1800,2,640]{2,0,1:T(8,128)(2,1)}, u32[]{:S(2)}, u32[]{:S(2)}) %collective-permute-start.1) | collective-permute-done | bytes 4608032 | tf_op jit(solution)/shard_map/ppermute | solution.py:24
  211.5 3.8 %broadcast_select_fusion = (bf16[1800,2,640]{2,0,1:T(8,128)(2,1)S(1)}, bf16[1800,2,640]{2,0,1:T(8,128)(2,1)S(1)}) fusion(bf16[1800,2,640]{2,0,1:T(8,128)(2,1)} %collective-permute-done.1, pred[]{:T(512)S(6)} %eq.27, bf16[900,2,640]{2,0,1:T(8,128)(2,1)S(1)} %copy-done.1, bf16[900,2,640]{2,0,1:T(8,128)(2,1)S(1)} %get-tuple-element.110), kind=kLoop, calls=%fused_computation.42 | loop fusion | flops 13824000 | bytes 18432000 | tf_op jit(solution)/shard_map/jit(_where)/select_n | solution.py:109
  215.3 10.8 %fusion.42 = (bf16[3600,640]{1,0:T(8,128)(2,1)}, bf16[3600,640]{1,0:T(8,128)(2,1)}) fusion(bf16[1800,2,640]{2,0,1:T(8,128)(2,1)S(1)} %get-tuple-element.108, bf16[1800,2,640]{2,0,1:T(8,128)(2,1)S(1)} %get-tuple-element.109), kind=kLoop, calls=%fused_computation.40 | loop fusion | flops 18432000 | bytes 18432000 | tf_op jit(solution)/shard_map/squeeze | solution.py:123
  226.1 15.2 %multiply_reduce_fusion = (f32[900]{0:T(1024)S(1)}, f32[900,640]{1,0:T(8,128)}) fusion(bf16[5120,640]{1,0:T(8,128)(2,1)} %all-gather.2.cloned.1.call-done, bf16[900,5120]{1,0:T(8,128)(2,1)} %param.11, f32[5120]{0:T(1024)S(1)} %copy-done.4, f32[5120]{0:T(1024)S(1)} %broadcast_add_fusion, f32[900]{0:T(1024)S(1)} %get-tuple-element.117, ...), kind=kOutput, calls=%fused_computation.45 | convolution fusion | flops 5927038976 | bytes 18125360 | tf_op jit(solution)/shard_map/dot_general | solution.py:86
  241.3 6.6 %psum.7 = f32[900]{0:T(1024)S(1)} all-reduce(f32[900]{0:T(1024)S(1)} %get-tuple-element.118), channel_id=1, replica_groups=mesh['tile'=8,'head'=4] {'head'}, use_global_device_ids=true, to_apply=%region_3.0 | all-reduce | flops 900 | bytes 7200 | tf_op jit(solution)/shard_map/psum | solution.py:91
  247.9 1.9 multiply_multiply_fusion
  249.9 2.4 copy.33
  252.3 3.3 reshape_reshape.3
  255.6 3.6 %subtract_convert_fusion = (bf16[900,5,64,1]{0,3,2,1:T(2,128)(2,1)S(1)}, bf16[900,5,64,1]{0,3,2,1:T(2,128)(2,1)S(1)}) fusion(f32[900,5,64,2]{0,3,2,1:T(2,128)S(1)} %reshape_reshape.3, f32[900,64]{0,1:T(8,128)S(1)} %get-tuple-element.115, f32[900,64]{0,1:T(8,128)S(1)} %get-tuple-element.114), kind=kLoop, calls=%fused_computation.50 | loop fusion | flops 2304000 | bytes 3916800 | tf_op jit(solution)/shard_map/convert
  259.2 3.0 pad_maximum_fusion.2
  262.2 1.0 convert_element_type.59
  263.3 1.1 copy.38
  264.4 67.7 %while.11 = (s32[]{:T(128)}, bf16[5,900,128]{2,1,0:T(8,128)(2,1)}, s32[5]{0:T(128)S(1)}, bf16[900,640]{1,0:T(8,128)(2,1)S(1)}, bf16[3600,640]{1,0:T(8,128)(2,1)}...) while((s32[]{:T(128)}, bf16[5,900,128]{2,1,0:T(8,128)(2,1)}, ...), condition=%wide.region_8.9_spmd.clone, body=%wide.region_5.8_spmd.clone.sunk | while | flops 1701232128 | bytes 41227864 | solution.py:145
  264.6 0.7 dynamic_slice.38
  266.1 0.1 broadcast_in_dim.183
  266.2 3.5 %fusion.65 = (f32[900]{0:T(1024)S(1)}, f32[900,3600]{1,0:T(8,128)S(1)}) fusion(pred[3600]{0:T(1024)(128)(4,1)S(1)} %broadcast_in_dim.183, bf16[3600,640]{1,0:T(8,128)(2,1)} %get-tuple-element.197, s32[]{:T(128)S(6)} %select_n.239, bf16[900,640]{1,0:T(8,128)(2,1)S(1)} %get-tuple-element.196), kind=kOutput, calls=%fused_computation.3.clone.1 | convolution fusion | flops 839159104 | bytes 14121744 | tf_op jit(solution)/shard_map/while/body/eval_jaxpr/dot_general | solution.py:132
  269.7 3.6 %fusion.66 = f32[900]{0:T(1024)S(1)} fusion(f32[900,3600]{1,0:T(8,128)S(1)} %get-tuple-element.169, f32[900]{0:T(1024)S(1)} %get-tuple-element.170, pred[3600]{0:T(1024)(128)(4,1)S(1)} %broadcast_in_dim.183), kind=kLoop, calls=%fused_computation.4.clone.1 | loop fusion | flops 16199100 | bytes 12970800 | tf_op jit(solution)/shard_map/while/body/eval_jaxpr/reduce_sum | solution.py:140
  273.4 4.7 %fusion.67 = bf16[5,900,128]{2,1,0:T(8,128)(2,1)} fusion(bf16[5,900,128]{2,1,0:T(8,128)(2,1)} %get-tuple-element.183, s32[]{:T(128)} %get-tuple-element.182, f32[900,3600]{1,0:T(8,128)S(1)} %get-tuple-element.169, f32[900]{0:T(1024)S(1)} %get-tuple-element.170, pred[3600]{0:T(1024)(128)(4,1)S(1)} %broadcast_in_dim.183, ...), kind=kOutput, calls=%fused_computation.11.clone.1 | convolution fusion | flops 845870400 | bytes 14124340 | tf_op jit(solution)/shard_map/while/body/eval_jaxpr/dot_general | solution.py:142
  278.1 0.7 dynamic_slice.38
  279.5 0.1 broadcast_in_dim.183
  279.6 3.6 %fusion.65 = (f32[900]{0:T(1024)S(1)}, f32[900,3600]{1,0:T(8,128)S(1)}) fusion(pred[3600]{0:T(1024)(128)(4,1)S(1)} %broadcast_in_dim.183, bf16[3600,640]{1,0:T(8,128)(2,1)} %get-tuple-element.197, s32[]{:T(128)S(6)} %select_n.239, bf16[900,640]{1,0:T(8,128)(2,1)S(1)} %get-tuple-element.196), kind=kOutput, calls=%fused_computation.3.clone.1 | convolution fusion | flops 839159104 | bytes 14121744 | tf_op jit(solution)/shard_map/while/body/eval_jaxpr/dot_general | solution.py:132
  283.2 3.6 %fusion.66 = f32[900]{0:T(1024)S(1)} fusion(f32[900,3600]{1,0:T(8,128)S(1)} %get-tuple-element.169, f32[900]{0:T(1024)S(1)} %get-tuple-element.170, pred[3600]{0:T(1024)(128)(4,1)S(1)} %broadcast_in_dim.183), kind=kLoop, calls=%fused_computation.4.clone.1 | loop fusion | flops 16199100 | bytes 12970800 | tf_op jit(solution)/shard_map/while/body/eval_jaxpr/reduce_sum | solution.py:140
  286.8 4.7 %fusion.67 = bf16[5,900,128]{2,1,0:T(8,128)(2,1)} fusion(bf16[5,900,128]{2,1,0:T(8,128)(2,1)} %get-tuple-element.183, s32[]{:T(128)} %get-tuple-element.182, f32[900,3600]{1,0:T(8,128)S(1)} %get-tuple-element.169, f32[900]{0:T(1024)S(1)} %get-tuple-element.170, pred[3600]{0:T(1024)(128)(4,1)S(1)} %broadcast_in_dim.183, ...), kind=kOutput, calls=%fused_computation.11.clone.1 | convolution fusion | flops 845870400 | bytes 14124340 | tf_op jit(solution)/shard_map/while/body/eval_jaxpr/dot_general | solution.py:142
  291.6 0.7 dynamic_slice.38
  293.0 0.1 broadcast_in_dim.183
  293.1 3.5 %fusion.65 = (f32[900]{0:T(1024)S(1)}, f32[900,3600]{1,0:T(8,128)S(1)}) fusion(pred[3600]{0:T(1024)(128)(4,1)S(1)} %broadcast_in_dim.183, bf16[3600,640]{1,0:T(8,128)(2,1)} %get-tuple-element.197, s32[]{:T(128)S(6)} %select_n.239, bf16[900,640]{1,0:T(8,128)(2,1)S(1)} %get-tuple-element.196), kind=kOutput, calls=%fused_computation.3.clone.1 | convolution fusion | flops 839159104 | bytes 14121744 | tf_op jit(solution)/shard_map/while/body/eval_jaxpr/dot_general | solution.py:132
  296.7 3.6 %fusion.66 = f32[900]{0:T(1024)S(1)} fusion(f32[900,3600]{1,0:T(8,128)S(1)} %get-tuple-element.169, f32[900]{0:T(1024)S(1)} %get-tuple-element.170, pred[3600]{0:T(1024)(128)(4,1)S(1)} %broadcast_in_dim.183), kind=kLoop, calls=%fused_computation.4.clone.1 | loop fusion | flops 16199100 | bytes 12970800 | tf_op jit(solution)/shard_map/while/body/eval_jaxpr/reduce_sum | solution.py:140
  300.3 4.7 %fusion.67 = bf16[5,900,128]{2,1,0:T(8,128)(2,1)} fusion(bf16[5,900,128]{2,1,0:T(8,128)(2,1)} %get-tuple-element.183, s32[]{:T(128)} %get-tuple-element.182, f32[900,3600]{1,0:T(8,128)S(1)} %get-tuple-element.169, f32[900]{0:T(1024)S(1)} %get-tuple-element.170, pred[3600]{0:T(1024)(128)(4,1)S(1)} %broadcast_in_dim.183, ...), kind=kOutput, calls=%fused_computation.11.clone.1 | convolution fusion | flops 845870400 | bytes 14124340 | tf_op jit(solution)/shard_map/while/body/eval_jaxpr/dot_general | solution.py:142
  305.1 0.7 dynamic_slice.38
  306.6 3.6 %fusion.65 = (f32[900]{0:T(1024)S(1)}, f32[900,3600]{1,0:T(8,128)S(1)}) fusion(pred[3600]{0:T(1024)(128)(4,1)S(1)} %broadcast_in_dim.183, bf16[3600,640]{1,0:T(8,128)(2,1)} %get-tuple-element.197, s32[]{:T(128)S(6)} %select_n.239, bf16[900,640]{1,0:T(8,128)(2,1)S(1)} %get-tuple-element.196), kind=kOutput, calls=%fused_computation.3.clone.1 | convolution fusion | flops 839159104 | bytes 14121744 | tf_op jit(solution)/shard_map/while/body/eval_jaxpr/dot_general | solution.py:132
  310.1 3.6 %fusion.66 = f32[900]{0:T(1024)S(1)} fusion(f32[900,3600]{1,0:T(8,128)S(1)} %get-tuple-element.169, f32[900]{0:T(1024)S(1)} %get-tuple-element.170, pred[3600]{0:T(1024)(128)(4,1)S(1)} %broadcast_in_dim.183), kind=kLoop, calls=%fused_computation.4.clone.1 | loop fusion | flops 16199100 | bytes 12970800 | tf_op jit(solution)/shard_map/while/body/eval_jaxpr/reduce_sum | solution.py:140
  313.8 4.7 %fusion.67 = bf16[5,900,128]{2,1,0:T(8,128)(2,1)} fusion(bf16[5,900,128]{2,1,0:T(8,128)(2,1)} %get-tuple-element.183, s32[]{:T(128)} %get-tuple-element.182, f32[900,3600]{1,0:T(8,128)S(1)} %get-tuple-element.169, f32[900]{0:T(1024)S(1)} %get-tuple-element.170, pred[3600]{0:T(1024)(128)(4,1)S(1)} %broadcast_in_dim.183, ...), kind=kOutput, calls=%fused_computation.11.clone.1 | convolution fusion | flops 845870400 | bytes 14124340 | tf_op jit(solution)/shard_map/while/body/eval_jaxpr/dot_general | solution.py:142
  318.5 0.7 dynamic_slice.38
  320.0 0.1 broadcast_in_dim.183
  320.1 3.6 %fusion.65 = (f32[900]{0:T(1024)S(1)}, f32[900,3600]{1,0:T(8,128)S(1)}) fusion(pred[3600]{0:T(1024)(128)(4,1)S(1)} %broadcast_in_dim.183, bf16[3600,640]{1,0:T(8,128)(2,1)} %get-tuple-element.197, s32[]{:T(128)S(6)} %select_n.239, bf16[900,640]{1,0:T(8,128)(2,1)S(1)} %get-tuple-element.196), kind=kOutput, calls=%fused_computation.3.clone.1 | convolution fusion | flops 839159104 | bytes 14121744 | tf_op jit(solution)/shard_map/while/body/eval_jaxpr/dot_general | solution.py:132
  323.6 3.6 %fusion.66 = f32[900]{0:T(1024)S(1)} fusion(f32[900,3600]{1,0:T(8,128)S(1)} %get-tuple-element.169, f32[900]{0:T(1024)S(1)} %get-tuple-element.170, pred[3600]{0:T(1024)(128)(4,1)S(1)} %broadcast_in_dim.183), kind=kLoop, calls=%fused_computation.4.clone.1 | loop fusion | flops 16199100 | bytes 12970800 | tf_op jit(solution)/shard_map/while/body/eval_jaxpr/reduce_sum | solution.py:140
  327.3 4.7 %fusion.67 = bf16[5,900,128]{2,1,0:T(8,128)(2,1)} fusion(bf16[5,900,128]{2,1,0:T(8,128)(2,1)} %get-tuple-element.183, s32[]{:T(128)} %get-tuple-element.182, f32[900,3600]{1,0:T(8,128)S(1)} %get-tuple-element.169, f32[900]{0:T(1024)S(1)} %get-tuple-element.170, pred[3600]{0:T(1024)(128)(4,1)S(1)} %broadcast_in_dim.183, ...), kind=kOutput, calls=%fused_computation.11.clone.1 | convolution fusion | flops 845870400 | bytes 14124340 | tf_op jit(solution)/shard_map/while/body/eval_jaxpr/dot_general | solution.py:142
  332.0 1.6 copy.39
  333.6 1.4 copy.40
  (30 shorter events, 0.7 us)
Async XLA Ops:
  6.5 219.5 %all-gather.2.cloned.1.call-start = ((), (), s32[]{:S(2)}) async-start(), calls=%async_computation | async-start | bytes 7372800 | tf_op jit(solution)/shard_map/all_gather | solution.py:88
  7.3 67.9 %collective-permute-start = (bf16[900,2,640]{2,1,0:T(2,128)(2,1)}, bf16[900,2,640]{2,1,0:T(2,128)(2,1)}, u32[]{:S(2)}, u32[]{:S(2)}) collective-permute-start(bf16[900,2,640]{2,1,0:T(2,128)(2,1)} %param.16), channel_id=1, source_target_pairs={{0,4},{4,0},{8,12},{12,8},{16,20},{20,16},{24,28},{28,24},{1,5},{5... | collective-permute-start | bytes 6912008 | tf_op jit(solution)/shard_map/ppermute | solution.py:24
  78.3 3.0 copy-start
  78.3 4.8 %copy-start.5 = (s32[8]{0:T(128)S(1)}, s32[8]{0:T(128)}, u32[]{:S(2)}) copy-start(s32[8]{0:T(128)} %param.17) | copy-start | bytes 100
  81.3 130.2 %collective-permute-start.1 = (bf16[1800,2,640]{2,0,1:T(8,128)(2,1)}, bf16[1800,2,640]{2,0,1:T(8,128)(2,1)}, u32[]{:S(2)}, u32[]{:S(2)}) collective-permute-start(bf16[1800,2,640]{2,0,1:T(8,128)(2,1)} %pad_maximum_fusion.1), channel_id=1, source_target_pairs={{0,8},{4,12},{8,0},{12,4},{16,24},{20,28},{24,16},{28,20},{1,9},{5... | collective-permute-start | bytes 13824008 | tf_op jit(solution)/shard_map/ppermute | solution.py:24
  83.4 6.6 %copy-start.2 = (f32[5120]{0:T(1024)S(1)}, f32[5120]{0:T(1024)}, u32[]{:S(2)}) copy-start(f32[5120]{0:T(1024)} %param.14) | copy-start | bytes 61444
  83.4 128.2 %copy-start.1 = (bf16[900,2,640]{2,0,1:T(8,128)(2,1)S(1)}, bf16[900,2,640]{2,0,1:T(8,128)(2,1)}, u32[]{:S(2)}) copy-start(bf16[900,2,640]{2,0,1:T(8,128)(2,1)} %copy-done) | copy-start | bytes 6912004
  215.3 10.8 %copy-start.4 = (f32[5120]{0:T(1024)S(1)}, f32[5120]{0:T(1024)}, u32[]{:S(2)}) copy-start(f32[5120]{0:T(1024)} %param.13) | copy-start | bytes 61444
  226.1 21.9 %copy-start.3 = (f32[640]{0:T(1024)S(1)}, f32[640]{0:T(1024)}, u32[]{:S(2)}) copy-start(f32[640]{0:T(1024)} %param.15) | copy-start | bytes 7684
Sparse Core Ops, SparseCore 0:
  9.5 130.7 all-gather.1
where the time goes:
time: 343 us; the launch traced here: 342 us
  waiting for transfers between devices  187 us (55%)
  matrix products  56.7 us (17%)
  other arithmetic  55.6 us (16%)
  local copies, waits for them, and re-layouts  14.7 us (4%)
  between operations  14.2 us (4%)
  blocking collectives  6.61 us (2%)
  loops' own time  3.83 us (1%)
    ppermute x2, waiting for transfers between devices, from_partner(): return lax.ppermute(value, axis, pairs)  186 us
    dot_general x5, matrix products, one_head(): mixed = jnp.dot(rounded, value_part, preferred_element_type=jnp.float32)  23.7 us
    reduce_sum x5, other arithmetic, one_head(): totals = jnp.sum(weights, axis=1, keepdims=True)  18.2 us
    dot_general x5, matrix products, one_head(): lax.dot_general(query_part, key_part, (((1,), (1,)), ((), ())), preferred...  17.7 us
    dot_general x1, matrix products, per_device(): jnp.dot(normed, lax.all_gather(query_weight, 'tile', axis=0, tiled=True),...  15.2 us
    squeeze x1, other arithmetic, per_device(): values_all = cache_rows[:, 1, :]  10.8 us
  transfers between devices with their start and end apart: 3, of which 2 were waited for; matrix products, arithmetic and copies ran while one was open for 8% of the time, Pallas kernels for 0%

commit v1 on v0

--- a/solution.py
+++ b/solution.py
@@ -1,9 +1,12 @@
+import functools
 import math
 
 import jax
 import jax.numpy as jnp
 import numpy as np
 from jax import lax
+from jax.experimental import pallas as pl
+from jax.experimental.pallas import tpu as pltpu
 from jax.sharding import PartitionSpec as P
 
 D = 5120
@@ -146,6 +149,393 @@
     return jnp.transpose(per_head, (1, 0, 2)).reshape(token_count, width_here)
 
 
+MESH = pl.DeviceIdType.MESH
+LANES = 128
+Z_ORDER = ((0, 1, 2, 3), (1, 0, 2, 3), (2, 3, 1, 0), (3, 2, 1, 0))
+STEPS = ((0, 1), (1, 1), (0, 0), (2, 1), (1, 0), (3, 1), (2, 0), (3, 0))
+
+
+def pick(index, values):
+    out = jnp.int32(values[-1])
+    for place in range(len(values) - 1):
+        out = jnp.where(index == place, jnp.int32(values[place]), out)
+    return out
+
+
+def project_kernel(
+    lat_ref, w_ref, shift_ref, scale_ref, gain_ref, k_ref, v_ref, group_ref,
+    q_ref, k_all, v_all,
+    lat, wbuf, acc, part, mean_s, rstd_s, cos_s, sin_s, rot, sq,
+    lat_sem, w_local, w_recv, w_sendy, w_sendr, w_sendl,
+    sq_recv, sq_send, q_send, q_recv, kv_recv, kv_y, kv_z, kv_relay, kv_sib,
+):
+    tile = lax.axis_index("tile")
+    head = lax.axis_index("head")
+    z, y = tile // 2, tile % 2
+    core = head % 2
+    zlow = z % 2
+    tile_y = z * 2 + (1 - y)
+    head_sib = head - core + (1 - core)
+    zpair = z - zlow + (1 - zlow)
+    tile_zp = zpair * 2 + y
+    own = zlow * 2 + y
+    own_y = zlow * 2 + (1 - y)
+    far = (1 - zlow) * 2 + y
+    far_y = (1 - zlow) * 2 + (1 - y)
+    rows = lat.shape[0]
+    depth = w_ref.shape[0]
+    is_main = core == y
+    not_main = core != y
+    heads_here = acc.shape[1] // LANES
+
+    def remote(src, dst, ssem, rsem, tile_to, head_to):
+        return pltpu.make_async_remote_copy(
+            src_ref=src, dst_ref=dst, send_sem=ssem, recv_sem=rsem,
+            device_id=(tile_to, head_to), device_id_type=MESH,
+        )
+
+    def greet(tile_to, head_to):
+        pl.semaphore_signal(
+            barrier, inc=1, device_id=(tile_to, head_to), device_id_type=MESH
+        )
+
+    barrier = pltpu.get_barrier_semaphore()
+    greet(tile_y, head)
+    greet(tile_y, head_sib)
+    for other in range(1, 4):
+        greet(tile, (head + other) % 4)
+    pl.when(z > 0)(lambda: greet(tile - 2, head))
+    pl.when(z < 3)(lambda: greet(tile + 2, head))
+    lat_copy = pltpu.make_async_copy(lat_ref, lat, lat_sem)
+    lat_copy.start()
+    w_copy = pltpu.make_async_copy(w_ref, wbuf.at[tile], w_local)
+    w_copy.start()
+    pl.semaphore_wait(barrier, 5 + pick(z, (1, 2, 2, 1)))
+
+    def send_y(zk):
+        slot = zk * 2 + y
+        return remote(wbuf.at[slot], wbuf.at[slot], w_sendy.at[zk], w_recv.at[slot], tile_y, head)
+
+    def send_right(zk):
+        slot = zk * 2 + y
+        return remote(wbuf.at[slot], wbuf.at[slot], w_sendr.at[zk], w_recv.at[slot], tile + 2, head)
+
+    def send_left(zk):
+        slot = zk * 2 + y
+        return remote(wbuf.at[slot], wbuf.at[slot], w_sendl.at[zk], w_recv.at[slot], tile - 2, head)
+
+    def forward(zk):
+        pl.when(jnp.logical_and(zk <= z, z < 3))(lambda: send_right(zk).start())
+        pl.when(jnp.logical_and(zk >= z, z > 0))(lambda: send_left(zk).start())
+        send_y(zk).start()
+
+    kv = ((k_ref, k_all), (v_ref, v_all))
+
+    def kv_local(i):
+        return pltpu.make_async_copy(kv[i][0], kv[i][1].at[own], kv_recv.at[i, own])
+
+    def kv_to_y(i):
+        return remote(kv[i][0], kv[i][1].at[own], kv_y.at[i], kv_recv.at[i, own], tile_y, head)
+
+    def kv_to_z(i):
+        return remote(kv[i][0], kv[i][1].at[own], kv_z.at[i], kv_recv.at[i, own], tile_zp, head)
+
+    def kv_to_relay(i):
+        return remote(
+            kv[i][1].at[own_y], kv[i][1].at[own_y], kv_relay.at[i], kv_recv.at[i, own_y],
+            tile_zp, head,
+        )
+
+    def kv_to_sib(i, slot):
+        src = kv[i][0] if slot is own else kv[i][1].at[slot]
+        return remote(
+            src, kv[i][1].at[slot], kv_sib.at[i, slot], kv_recv.at[i, slot], tile, head_sib
+        )
+
+    def kv_wait(i, slot):
+        remote(
+            kv[i][1].at[slot], kv[i][1].at[slot], kv_sib.at[i, slot], kv_recv.at[i, slot],
+            tile, head_sib,
+        ).wait_recv()
+
+    w_copy.wait()
+    forward(z)
+    lat_copy.wait()
+
+    part[...] = jnp.zeros_like(part)
+    acc[:, :LANES] = jnp.zeros_like(part)
+
+    def columns(i):
+        return pl.ds(pl.multiple_of(i * LANES, LANES), LANES)
+
+    @pl.loop(0, D // LANES)
+    def _(i):
+        x = lat[:, columns(i)].astype(jnp.float32)
+        part[...] += x
+        acc[:, :LANES] += x * x
+
+    mean = jnp.sum(part[...], axis=1, keepdims=True) / D
+    var = jnp.sum(acc[:, :LANES], axis=1, keepdims=True) / D - mean * mean
+    mean_s[...] = jnp.broadcast_to(mean, mean_s.shape)
+    rstd_s[...] = jnp.broadcast_to(lax.rsqrt(var + norm_eps), rstd_s.shape)
+
+    @pl.loop(0, D // LANES)
+    def _(i):
+        x = lat[:, columns(i)].astype(jnp.float32)
+        normed = (x - mean_s[...]) * rstd_s[...] * (1.0 + scale_ref[:, columns(i)])
+        lat[:, columns(i)] = (normed + shift_ref[:, columns(i)]).astype(jnp.bfloat16)
+
+    lane = lax.broadcasted_iota(jnp.int32, (1, LANES), 1)
+    pair = lane // 2
+    space_pairs = HD // 6
+    time_pairs = HD // 2 - 2 * space_pairs
+    in_time = pair < time_pairs
+    in_height = pair < time_pairs + space_pairs
+    offset = jnp.where(
+        in_time, pair, jnp.where(in_height, pair - time_pairs, pair - time_pairs - space_pairs)
+    )
+    extent = jnp.where(in_time, jnp.float32(time_pairs), jnp.float32(space_pairs))
+    theta = jnp.exp(-math.log(10000.0) * offset.astype(jnp.float32) / extent)
+    token = (
+        own * rows + lax.broadcasted_iota(jnp.int32, (rows, LANES), 0)
+    ).astype(jnp.float32)
+    frame = jnp.floor((token + 0.5) * (1.0 / (GH * GW)))
+    in_frame = token - frame * (GH * GW)
+    height = jnp.floor((in_frame + 0.5) * (1.0 / GW))
+    width = in_frame - height * GW
+    time = (group_ref[0] * FRAMES).astype(jnp.float32) + frame
+    position = jnp.where(in_time, time, jnp.where(in_height, height, width))
+    angle = position * theta
+    even = lane % 2 == 0
+    cos_s[...] = jnp.cos(angle)
+    sine = jnp.sin(angle)
+    sin_s[...] = jnp.where(even, -sine, sine)
+
+    acc[...] = jnp.zeros_like(acc)
+
+    @pl.loop(0, 8)
+    def _(e):
+        k = pick(e, [s[0] for s in STEPS])
+        along_z = pick(e, [s[1] for s in STEPS])
+        zk = jnp.where(
+            z == 0, pick(k, Z_ORDER[0]),
+            jnp.where(z == 1, pick(k, Z_ORDER[1]),
+                      jnp.where(z == 2, pick(k, Z_ORDER[2]), pick(k, Z_ORDER[3]))),
+        )
+        slot = zk * 2 + jnp.where(along_z == 1, y, 1 - y)
+
+        @pl.when(e > 0)
+        def _():
+            remote(
+                wbuf.at[slot], wbuf.at[slot], w_sendy.at[zk], w_recv.at[slot], tile_y, head
+            ).wait_recv()
+
+        @pl.when(jnp.logical_and(e > 0, along_z == 1))
+        def _():
+            forward(zk)
+
+        @pl.when(e == 5)
+        def _():
+            @pl.when(is_main)
+            def _():
+                for i in range(2):
+                    kv_to_z(i).start()
+                    kv_local(i).start()
+                    kv_to_sib(i, own).start()
+
+            @pl.when(not_main)
+            def _():
+                for i in range(2):
+                    kv_to_y(i).start()
+
+        cols = pl.ds(pl.multiple_of(slot * depth, LANES), depth)
+        acc[...] += jnp.dot(lat[:, cols], wbuf[slot], preferred_element_type=jnp.float32)
+
+    total = jnp.zeros((rows, LANES), jnp.float32)
+    for h in range(heads_here):
+        x = acc[:, h * LANES:(h + 1) * LANES]
+        total = total + x * x
+    part[...] = total
+    sq[head] = lax.dot_general(
+        jnp.ones((8, LANES), jnp.float32), part[...], (((1,), (1,)), ((), ())),
+        preferred_element_type=jnp.float32, precision=lax.Precision.HIGHEST,
+    )
+
+    def sq_copy(other, slot):
+        return remote(
+            sq.at[slot], sq.at[slot], sq_send.at[other - 1], sq_recv.at[slot],
+            tile, (head + other) % 4,
+        )
+
+    for other in range(1, 4):
+        sq_copy(other, head).start()
+    for other in range(1, 4):
+        sq_copy(other, (head + other) % 4).wait_recv()
+    for other in range(1, 4):
+        sq_copy(other, head).wait_send()
+    summed = sq[0] + sq[1] + sq[2] + sq[3]
+    first = (lax.broadcasted_iota(jnp.int32, (8, LANES), 0) == 0).astype(jnp.float32)
+    spread = lax.dot_general(
+        summed, first, (((0,), (0,)), ((), ())),
+        preferred_element_type=jnp.float32, precision=lax.Precision.HIGHEST,
+    )
+    rstd_s[...] = lax.rsqrt(spread / (HEADS * HD) + norm_eps)
+    for h in range(heads_here):
+        cut = slice(h * LANES, (h + 1) * LANES)
+        x = acc[:, cut] * rstd_s[...] * gain_ref[:, cut]
+        turned = jnp.where(
+            even, pltpu.roll(x, LANES - 1, 1), pltpu.roll(x, 1, 1)
+        )
+        rot[:, cut] = (x * cos_s[...] + turned * sin_s[...]).astype(jnp.bfloat16)
+
+    def q_out():
+        return remote(rot, q_ref, q_send, q_recv, tile_y, head_sib)
+
+    def q_stay():
+        return pltpu.make_async_copy(rot, q_ref, q_recv)
+
+    pl.when(not_main)(lambda: q_out().start())
+    pl.when(is_main)(lambda: q_stay().start())
+
+    @pl.when(is_main)
+    def _():
+        for i in range(2):
+            kv_wait(i, own_y)
+            kv_to_relay(i).start()
+            kv_to_sib(i, own_y).start()
+        for i in range(2):
+            kv_wait(i, far)
+            kv_to_sib(i, far).start()
+        for i in range(2):
+            kv_wait(i, far_y)
+            kv_to_sib(i, far_y).start()
+        for i in range(2):
+            kv_local(i).wait()
+            kv_to_z(i).wait_send()
+            kv_to_relay(i).wait_send()
+            for slot in (own, own_y, far, far_y):
+                kv_to_sib(i, slot).wait_send()
+        q_stay().wait()
+
+    @pl.when(not_main)
+    def _():
+        for i in range(2):
+            kv_to_y(i).wait_send()
+            for slot in (own, own_y, far, far_y):
+                kv_wait(i, slot)
+        q_out().wait_send()
+        q_out().wait_recv()
+
+    for zk in range(4):
+        send_y(zk).wait_send()
+        pl.when(jnp.logical_and(zk <= z, z < 3))(lambda: send_right(zk).wait_send())
+        pl.when(jnp.logical_and(zk >= z, z > 0))(lambda: send_left(zk).wait_send())
+
+
+def project(latents, query_weight, mod_shift, mod_scale, query_gain, keys, values, group_index):
+    rows, width = latents.shape[0], query_weight.shape[1]
+    any_spec = pl.BlockSpec(memory_space=pl.ANY)
+    vmem = pl.BlockSpec(memory_space=pltpu.VMEM)
+    dma = pltpu.SemaphoreType.DMA
+    wide = pltpu.VMEM((rows, LANES), jnp.float32)
+    return pl.pallas_call(
+        project_kernel,
+        out_shape=(
+            jax.ShapeDtypeStruct((rows, width), jnp.bfloat16),
+            jax.ShapeDtypeStruct((4, rows, width), jnp.bfloat16),
+            jax.ShapeDtypeStruct((4, rows, width), jnp.bfloat16),
+        ),
+        in_specs=[
+            any_spec, any_spec, vmem, vmem, vmem, any_spec, any_spec,
+            pl.BlockSpec(memory_space=pltpu.SMEM),
+        ],
+        out_specs=(any_spec, any_spec, any_spec),
+        scratch_shapes=[
+            pltpu.VMEM((rows, D), jnp.bfloat16),
+            pltpu.VMEM((8,) + query_weight.shape, jnp.bfloat16),
+            pltpu.VMEM((rows, width), jnp.float32),
+            wide, wide, wide, wide, wide,
+            pltpu.VMEM((rows, width), jnp.bfloat16),
+            pltpu.VMEM((4, 8, rows), jnp.float32),
+            dma(()), dma(()), dma((8,)), dma((4,)), dma((4,)), dma((4,)),
+            dma((4,)), dma((3,)), dma(()), dma(()),
+            dma((2, 4)), dma((2,)), dma((2,)), dma((2,)), dma((2, 4)),
+        ],
+        compiler_params=pltpu.CompilerParams(
+            collective_id=0, has_side_effects=True, vmem_limit_bytes=60 * 2**20
+        ),
+    )(
+        latents, query_weight, mod_shift[None], mod_scale[None], query_gain[None],
+        keys, values, group_index,
+    )
+
+
+def attend_kernel(counts_ref, q_ref, k_ref, v_ref, o_ref):
+    span, slots = k_ref.shape[0], k_ref.shape[1]
+    factor = math.log2(math.e) / math.sqrt(HD)
+    query = q_ref[...]
+    place = lax.broadcasted_iota(jnp.int32, (1, slots), 1)
+    scores = []
+    for j in range(span):
+        raw = lax.dot_general(
+            query, k_ref[j], (((1,), (1,)), ((), ())), preferred_element_type=jnp.float32
+        )
+        scores.append(jnp.where(place < counts_ref[j], raw, -1e30))
+    top = functools.reduce(
+        jnp.maximum, [jnp.max(s, axis=1, keepdims=True) for s in scores]
+    )
+    totals = jnp.zeros_like(top)
+    mixed = jnp.zeros(o_ref.shape, jnp.float32)
+    for j in range(span):
+        weights = jnp.exp2((scores[j] - top) * factor)
+        totals += jnp.sum(weights, axis=1, keepdims=True)
+        mixed += jnp.dot(
+            weights.astype(jnp.bfloat16), v_ref[j], preferred_element_type=jnp.float32
+        )
+    o_ref[...] = (mixed / totals).astype(jnp.bfloat16)
+
+
+def attend(counts, queries, keys, values):
+    rows, width = queries.shape
+    span = keys.shape[0]
+    block = 304
+    whole = pl.BlockSpec((span, rows, HD), lambda h, i: (0, 0, h))
+    return pl.pallas_call(
+        attend_kernel,
+        grid=(width // HD, pl.cdiv(rows, block)),
+        out_shape=jax.ShapeDtypeStruct((rows, width), jnp.bfloat16),
+        in_specs=[
+            pl.BlockSpec(memory_space=pltpu.SMEM),
+            pl.BlockSpec((block, HD), lambda h, i: (i, h)),
+            whole, whole,
+        ],
+        out_specs=pl.BlockSpec((block, HD), lambda h, i: (i, h)),
+        compiler_params=pltpu.CompilerParams(vmem_limit_bytes=48 * 2**20),
+    )(counts, queries, keys, values)
+
+
+def swap_pairs():
+    pairs = []
+    for tile in range(8):
+        for head in range(4):
+            here = tile * 4 + head
+            there = here if tile % 2 == head % 2 else (tile ^ 1) * 4 + (head ^ 1)
+            pairs.append((here, there))
+    return pairs
+
+
+def per_device_square(
+    latents, query_weight, mod_shift, mod_scale, query_gain, cache_blocks, block_counts, group_index
+):
+    keys, values = cache_blocks[:, 0, :], cache_blocks[:, 1, :]
+    queries, keys_all, values_all = project(
+        latents, query_weight, mod_shift, mod_scale, query_gain, keys, values, group_index
+    )
+    counts = lax.dynamic_slice_in_dim(block_counts, lax.axis_index("tile") // 4 * 4, 4)
+    attended = attend(counts, queries, keys_all, values_all)
+    return lax.ppermute(attended, ("tile", "head"), swap_pairs())
+
+
 def solution(mesh):
     in_specs = (
         P("tile", None),
@@ -158,6 +548,10 @@
         P(),
     )
     out_specs = P("tile", "head")
+    square = mesh.shape["tile"] == 8 and mesh.shape["head"] == 4
     return jax.shard_map(
-        per_device, mesh=mesh, in_specs=in_specs, out_specs=out_specs, check_vma=False
-    )
+        per_device_square if square else per_device, mesh=mesh,
+        in_specs=in_specs,
+        out_specs=out_specs,
+        check_vma=False,
+    )

time: 343 us -> 219 us (0.64)
  Pallas kernels: 0 us -> 183 us
  waiting for transfers between devices: 187 us -> 15.4 us
  matrix products: 56.7 us -> 0 us
  other arithmetic: 55.6 us -> 0 us
  between operations: 14.2 us -> 0.69 us
  blocking collectives: 6.61 us -> 0 us
  loops' own time: 3.83 us -> 0 us
    pallas_call x0 -> x2, Pallas kernels: none -> 183 us  [the longest x1 123 us: project(): pl.pallas_call(project_kernel, out_shape=(jax.ShapeDtypeStruct((rows, wid...]
    ppermute x2 -> x1, waiting for transfers between devices: 186 us -> 15.4 us  [per_device_square(): return lax.ppermute(attended, ('tile', 'head'), swap_pairs())]
    dot_general x11 -> x0, matrix products: 56.7 us -> none  [the longest x5 23.7 us: one_head(): mixed = jnp.dot(rounded, value_part, preferred_element_type=jnp.float32)]
    reduce_sum x7 -> x0, other arithmetic: 25 us -> none  [the longest x5 18.2 us: one_head(): totals = jnp.sum(weights, axis=1, keepdims=True)]
    squeeze x1 -> x0, other arithmetic: 10.8 us -> none  [per_device(): values_all = cache_rows[:, 1, :]]
    slice x0 -> x1, local copies, waits for them, and re-layouts: none -> 7.72 us  [per_device_square(): keys, values = (cache_blocks[:, 0, :], cache_blocks[:, 1, :])]
    select_n x2 -> x0, other arithmetic: 6.94 us -> none  [the longest x1 3.76 us: per_device(): upper_rows = jnp.where(mine_high, cache_rows, partner)]
    psum x1 -> x0, blocking collectives: 6.61 us -> none  [per_device(): squares = lax.psum(jnp.sum(queries * queries, axis=1), 'head')]
  transfers between devices with their start and end apart: 3 -> 1, of which waited for: 2 -> 1; matrix products, arithmetic and copies ran while one was open for 8% -> 0% of each run, Pallas kernels for 0% -> 0%
where the time goes in v1:
time: 219 us; the launch traced here: 216 us
  Pallas kernels  183 us (84%)
  waiting for transfers between devices  15.4 us (7%)
  local copies, waits for them, and re-layouts  14.7 us (7%)
    pallas_call x1, Pallas kernels, project(): pl.pallas_call(project_kernel, out_shape=(jax.ShapeDtypeStruct((rows, wid...  123 us
    pallas_call x1, Pallas kernels, attend(): pl.pallas_call(attend_kernel, grid=(width // HD, pl.cdiv(rows, block)), o...  60.3 us
    ppermute x1, waiting for transfers between devices, per_device_square(): return lax.ppermute(attended, ('tile', 'head'), swap_pairs())  15.4 us
    slice x1, local copies, waits for them, and re-layouts, per_device_square(): keys, values = (cache_blocks[:, 0, :], cache_blocks[:, 1, :])  7.72 us
  transfers between devices with their start and end apart: 1, of which 1 were waited for; matrix products, arithmetic and copies ran while one was open for 0% of the time, Pallas kernels for 0%

profile of v1, /device:TPU:1, one launch (start us, length us, event | category | flops | bytes accessed | tf_op | source)
XLA Modules:
  0.0 215.9 jit_solution(140763618838176423)
XLA Ops:
  0.7 1.3 broadcast_in_dim.11.gain_ref
  1.9 0.0 copy-start.1
  1.9 7.7 %fusion = (bf16[900,1,640]{2,1,0:T(2,128)(2,1)S(1)}, bf16[900,1,640]{2,1,0:T(2,128)(2,1)}) fusion(bf16[900,2,640]{2,1,0:T(2,128)(2,1)} %param.13), kind=kLoop, calls=%fused_computation.2 | loop fusion | bytes 4608000 | tf_op jit(solution)/shard_map/slice | solution.py:530
  9.6 0.0 copy-done.1
  9.6 0.1 dynamic_slice.3.counts_ref
  9.7 3.4 %copy_bitcast_fusion = (bf16[900,640]{1,0:T(8,128)(2,1)}, bf16[900,640]{1,0:T(8,128)(2,1)}) fusion(bf16[900,1,640]{2,1,0:T(2,128)(2,1)S(1)} %get-tuple-element.11, bf16[900,1,640]{2,1,0:T(2,128)(2,1)} %get-tuple-element.12), kind=kLoop, calls=%fused_computation | loop fusion | bytes 4608000 | tf_op jit(solution)/shard_map/squeeze | solution.py:530
  13.1 122.9 %shard_map.82 = (bf16[900,640]{1,0:T(8,128)(2,1)}, bf16[4,900,640]{2,1,0:T(8,128)(2,1)}, bf16[4,900,640]{2,1,0:T(8,128)(2,1)}) custom-call(bf16[900,5120]{1,0:T(8,128)(2,1)} %lat_ref.1, bf16[640,640]{1,0:T(8,128)(2,1)} %w_ref.1, f32[1,5120]{1,0:T(1,128)} %bitcast.6, f32[1,5120]{1,0:T(1,128)} %bitcast.7, f32[1,640]{1,0:T(1,128)} %broadcast_in_dim.11.gain_ref, ...), custom_call_target="tpu_custom_call" | custom-call | tf_op jit(solution)/shard_map/pallas_call | solution.py:441
  136.0 0.0 copy-start
  136.0 1.3 copy-done
  137.3 60.3 %shard_map.83 = bf16[900,640]{1,0:T(8,128)(2,1)S(1)} custom-call(s32[4]{0:T(128)S(1)} %dynamic_slice.3.counts_ref, bf16[900,640]{1,0:T(8,128)(2,1)S(1)} %copy-done, bf16[4,900,640]{2,1,0:T(8,128)(2,1)} %get-tuple-element.9.k_ref, bf16[4,900,640]{2,1,0:T(8,128)(2,1)} %get-tuple-element.10.v_ref), custom_call_target="tpu_custom_call" | custom-call | tf_op jit(solution)/shard_map/pallas_call | solution.py:503
  197.6 1.9 collective-permute-start
  199.5 15.4 %collective-permute-done = bf16[900,640]{1,0:T(8,128)(2,1)S(1)} collective-permute-done((bf16[900,640]{1,0:T(8,128)(2,1)S(1)}, bf16[900,640]{1,0:T(8,128)(2,1)S(1)}, u32[]{:S(2)}, u32[]{:S(2)}) %collective-permute-start) | collective-permute-done | bytes 1152032 | tf_op jit(solution)/shard_map/ppermute | solution.py:536
  214.9 1.0 copy.17
Async XLA Ops:
  1.9 7.7 %copy-start.1 = (s32[8]{0:T(128)S(1)}, s32[8]{0:T(128)}, u32[]{:S(2)}) copy-start(s32[8]{0:T(128)} %param.14) | copy-start | bytes 100
  136.0 1.3 copy-start
  197.6 17.3 %collective-permute-start = (bf16[900,640]{1,0:T(8,128)(2,1)S(1)}, bf16[900,640]{1,0:T(8,128)(2,1)S(1)}, u32[]{:S(2)}, u32[]{:S(2)}) collective-permute-start(bf16[900,640]{1,0:T(8,128)(2,1)S(1)} %shard_map.83), channel_id=1, source_target_pairs={{0,0},{1,4},{2,2},{3,6},{4,1},{5,5},{6,3},{7,7},{8,8},{9,12},{10,1... | collective-permute-start | bytes 3456008 | tf_op jit(solution)/shard_map/ppermute | solution.py:536

commit v2 on v1

--- a/solution.py
+++ b/solution.py
@@ -1,4 +1,3 @@
-import functools
 import math
 
 import jax
@@ -163,9 +162,11 @@
 
 
 def project_kernel(
-    lat_ref, w_ref, shift_ref, scale_ref, gain_ref, k_ref, v_ref, group_ref,
-    q_ref, k_all, v_all,
+    lat_ref, w_ref, shift_ref, scale_ref, gain_ref, cache_ref, counts_ref, group_ref,
+    o_ref,
     lat, wbuf, acc, part, mean_s, rstd_s, cos_s, sin_s, rot, sq,
+    cache, kv_own, kv_all, query, mixed, top, result,
+    cache_sem, o_send, o_recv,
     lat_sem, w_local, w_recv, w_sendy, w_sendr, w_sendl,
     sq_recv, sq_send, q_send, q_recv, kv_recv, kv_y, kv_z, kv_relay, kv_sib,
 ):
@@ -208,6 +209,8 @@
     pl.when(z < 3)(lambda: greet(tile + 2, head))
     lat_copy = pltpu.make_async_copy(lat_ref, lat, lat_sem)
     lat_copy.start()
+    cache_copy = pltpu.make_async_copy(cache_ref, cache, cache_sem)
+    cache_copy.start()
     w_copy = pltpu.make_async_copy(w_ref, wbuf.at[tile], w_local)
     w_copy.start()
     pl.semaphore_wait(barrier, 5 + pick(z, (1, 2, 2, 1)))
@@ -229,34 +232,26 @@
         pl.when(jnp.logical_and(zk >= z, z > 0))(lambda: send_left(zk).start())
         send_y(zk).start()
 
-    kv = ((k_ref, k_all), (v_ref, v_all))
-
-    def kv_local(i):
-        return pltpu.make_async_copy(kv[i][0], kv[i][1].at[own], kv_recv.at[i, own])
-
     def kv_to_y(i):
-        return remote(kv[i][0], kv[i][1].at[own], kv_y.at[i], kv_recv.at[i, own], tile_y, head)
+        return remote(
+            kv_own.at[i], kv_all.at[i, own], kv_y.at[i], kv_recv.at[i, own], tile_y, head
+        )
+
+    def kv_slot(i, slot, ssem, tile_to, head_to):
+        ref = kv_all.at[i, slot]
+        return remote(ref, ref, ssem, kv_recv.at[i, slot], tile_to, head_to)
 
     def kv_to_z(i):
-        return remote(kv[i][0], kv[i][1].at[own], kv_z.at[i], kv_recv.at[i, own], tile_zp, head)
+        return kv_slot(i, own, kv_z.at[i], tile_zp, head)
 
     def kv_to_relay(i):
-        return remote(
-            kv[i][1].at[own_y], kv[i][1].at[own_y], kv_relay.at[i], kv_recv.at[i, own_y],
-            tile_zp, head,
-        )
+        return kv_slot(i, own_y, kv_relay.at[i], tile_zp, head)
 
     def kv_to_sib(i, slot):
-        src = kv[i][0] if slot is own else kv[i][1].at[slot]
-        return remote(
-            src, kv[i][1].at[slot], kv_sib.at[i, slot], kv_recv.at[i, slot], tile, head_sib
-        )
+        return kv_slot(i, slot, kv_sib.at[i, slot], tile, head_sib)
 
     def kv_wait(i, slot):
-        remote(
-            kv[i][1].at[slot], kv[i][1].at[slot], kv_sib.at[i, slot], kv_recv.at[i, slot],
-            tile, head_sib,
-        ).wait_recv()
+        kv_to_sib(i, slot).wait_recv()
 
     w_copy.wait()
     forward(z)
@@ -284,6 +279,18 @@
         x = lat[:, columns(i)].astype(jnp.float32)
         normed = (x - mean_s[...]) * rstd_s[...] * (1.0 + scale_ref[:, columns(i)])
         lat[:, columns(i)] = (normed + shift_ref[:, columns(i)]).astype(jnp.bfloat16)
+
+    cache_copy.wait()
+
+    @pl.when(is_main)
+    def _():
+        kv_all[0, own] = cache[:, 0, :]
+        kv_all[1, own] = cache[:, 1, :]
+
+    @pl.when(not_main)
+    def _():
+        kv_own[0] = cache[:, 0, :]
+        kv_own[1] = cache[:, 1, :]
 
     lane = lax.broadcasted_iota(jnp.int32, (1, LANES), 1)
     pair = lane // 2
@@ -334,19 +341,16 @@
         def _():
             forward(zk)
 
-        @pl.when(e == 5)
-        def _():
-            @pl.when(is_main)
-            def _():
-                for i in range(2):
-                    kv_to_z(i).start()
-                    kv_local(i).start()
-                    kv_to_sib(i, own).start()
-
-            @pl.when(not_main)
-            def _():
-                for i in range(2):
-                    kv_to_y(i).start()
+        @pl.when(jnp.logical_and(e == 5, is_main))
+        def _():
+            for i in range(2):
+                kv_to_z(i).start()
+                kv_to_sib(i, own).start()
+
+        @pl.when(jnp.logical_and(e == 7, not_main))
+        def _():
+            for i in range(2):
+                kv_to_y(i).start()
 
         cols = pl.ds(pl.multiple_of(slot * depth, LANES), depth)
         acc[...] += jnp.dot(lat[:, cols], wbuf[slot], preferred_element_type=jnp.float32)
@@ -389,42 +393,122 @@
         rot[:, cut] = (x * cos_s[...] + turned * sin_s[...]).astype(jnp.bfloat16)
 
     def q_out():
-        return remote(rot, q_ref, q_send, q_recv, tile_y, head_sib)
-
-    def q_stay():
-        return pltpu.make_async_copy(rot, q_ref, q_recv)
+        return remote(rot, query, q_send, q_recv, tile_y, head_sib)
 
     pl.when(not_main)(lambda: q_out().start())
-    pl.when(is_main)(lambda: q_stay().start())
+
+    @pl.when(is_main)
+    def _():
+        query[...] = rot[...]
+        kv_wait(0, own_y)
+        kv_to_relay(0).start()
+        kv_to_sib(0, own_y).start()
+
+    @pl.when(not_main)
+    def _():
+        q_out().wait_send()
+        q_out().wait_recv()
+        for i in range(2):
+            kv_wait(i, own)
+
+    factor = math.log2(math.e) / math.sqrt(HD)
+    clip_first = tile // 4 * 4
+    kv_lane = lax.broadcasted_iota(jnp.int32, (rows, LANES), 1)
+    kv_row = lax.broadcasted_iota(jnp.int32, (rows, LANES), 0)
+    mark = jnp.where(kv_lane == 0, 1.0, 0.0).astype(jnp.bfloat16)
+    ones = jnp.ones((rows, LANES), jnp.bfloat16)
+    top[...] = jnp.full(top.shape, -1e30, jnp.float32)
+    mixed[...] = jnp.zeros_like(mixed)
+
+    def o_out(h):
+        cut = slice(h * LANES, (h + 1) * LANES)
+        return remote(
+            result.at[:, cut], o_ref.at[:, cut], o_send.at[h], o_recv.at[h], tile_y, head_sib
+        )
+
+    def o_stay(h):
+        cut = slice(h * LANES, (h + 1) * LANES)
+        return pltpu.make_async_copy(result.at[:, cut], o_ref.at[:, cut], o_recv.at[h])
+
+    def attend_tile(slot, last):
+        invalid = jnp.logical_and(kv_row >= counts_ref[clip_first + slot], kv_lane == 0)
+        bias = jnp.where(invalid, -1e30, 0.0).astype(jnp.bfloat16)
+
+        def score(h):
+            cut = slice(h * LANES, (h + 1) * LANES)
+            return lax.dot_general(
+                jnp.concatenate([query[:, cut], mark], axis=1),
+                jnp.concatenate([kv_all[0, slot, :, cut], bias], axis=1),
+                (((1,), (1,)), ((), ())), preferred_element_type=jnp.float32,
+            )
+
+        following = score(0)
+        for h in range(heads_here):
+            cut = slice(h * LANES, (h + 1) * LANES)
+            scores = following
+            if h + 1 < heads_here:
+                following = score(h + 1)
+            before = top[:, h:h + 1]
+            now = jnp.maximum(before, jnp.max(scores, axis=1, keepdims=True))
+            weights = jnp.exp2((scores - now) * factor).astype(jnp.bfloat16)
+            wide = slice(2 * h * LANES, 2 * (h + 1) * LANES)
+            value = mixed[:, wide] * jnp.exp2((before - now) * factor) + jnp.dot(
+                weights, jnp.concatenate([kv_all[1, slot, :, cut], ones], axis=1),
+                preferred_element_type=jnp.float32,
+            )
+            if last:
+                result[:, cut] = (value[:, :LANES] / value[:, LANES:]).astype(jnp.bfloat16)
+                pl.when(not_main)(lambda: o_out(h).start())
+                pl.when(is_main)(lambda: o_stay(h).start())
+            else:
+                top[:, h:h + 1] = now
+                mixed[:, wide] = value
+
+    @pl.loop(0, 3)
+    def _(t):
+        @pl.when(jnp.logical_and(t == 1, is_main))
+        def _():
+            kv_wait(1, own_y)
+            kv_to_relay(1).start()
+            kv_to_sib(1, own_y).start()
+
+        @pl.when(jnp.logical_and(t == 2, is_main))
+        def _():
+            for i in range(2):
+                kv_wait(i, far)
+                kv_to_sib(i, far).start()
+
+        slot = jnp.where(t == 0, own, jnp.where(t == 1, own_y, far))
+
+        @pl.when(jnp.logical_and(t > 0, not_main))
+        def _():
+            for i in range(2):
+                kv_wait(i, slot)
+
+        attend_tile(slot, False)
+
+    for i in range(2):
+        kv_wait(i, far_y)
+        pl.when(is_main)(lambda: kv_to_sib(i, far_y).start())
+    attend_tile(far_y, True)
 
     @pl.when(is_main)
     def _():
         for i in range(2):
-            kv_wait(i, own_y)
-            kv_to_relay(i).start()
-            kv_to_sib(i, own_y).start()
-        for i in range(2):
-            kv_wait(i, far)
-            kv_to_sib(i, far).start()
-        for i in range(2):
-            kv_wait(i, far_y)
-            kv_to_sib(i, far_y).start()
-        for i in range(2):
-            kv_local(i).wait()
             kv_to_z(i).wait_send()
             kv_to_relay(i).wait_send()
             for slot in (own, own_y, far, far_y):
                 kv_to_sib(i, slot).wait_send()
-        q_stay().wait()
+        for h in range(heads_here):
+            o_stay(h).wait()
 
     @pl.when(not_main)
     def _():
         for i in range(2):
             kv_to_y(i).wait_send()
-            for slot in (own, own_y, far, far_y):
-                kv_wait(i, slot)
-        q_out().wait_send()
-        q_out().wait_recv()
+        for h in range(heads_here):
+            o_out(h).wait_send()
+            o_out(h).wait_recv()
 
     for zk in range(4):
         send_y(zk).wait_send()
@@ -432,24 +516,20 @@
         pl.when(jnp.logical_and(zk >= z, z > 0))(lambda: send_left(zk).wait_send())
 
 
-def project(latents, query_weight, mod_shift, mod_scale, query_gain, keys, values, group_index):
+def project(
+    latents, query_weight, mod_shift, mod_scale, query_gain, cache_blocks, block_counts, group_index
+):
     rows, width = latents.shape[0], query_weight.shape[1]
     any_spec = pl.BlockSpec(memory_space=pl.ANY)
     vmem = pl.BlockSpec(memory_space=pltpu.VMEM)
+    smem = pl.BlockSpec(memory_space=pltpu.SMEM)
     dma = pltpu.SemaphoreType.DMA
     wide = pltpu.VMEM((rows, LANES), jnp.float32)
     return pl.pallas_call(
         project_kernel,
-        out_shape=(
-            jax.ShapeDtypeStruct((rows, width), jnp.bfloat16),
-            jax.ShapeDtypeStruct((4, rows, width), jnp.bfloat16),
-            jax.ShapeDtypeStruct((4, rows, width), jnp.bfloat16),
-        ),
-        in_specs=[
-            any_spec, any_spec, vmem, vmem, vmem, any_spec, any_spec,
-            pl.BlockSpec(memory_space=pltpu.SMEM),
-        ],
-        out_specs=(any_spec, any_spec, any_spec),
+        out_shape=jax.ShapeDtypeStruct((rows, width), jnp.bfloat16),
+        in_specs=[any_spec, any_spec, vmem, vmem, vmem, any_spec, smem, smem],
+        out_specs=any_spec,
         scratch_shapes=[
             pltpu.VMEM((rows, D), jnp.bfloat16),
             pltpu.VMEM((8,) + query_weight.shape, jnp.bfloat16),
@@ -457,83 +537,25 @@
             wide, wide, wide, wide, wide,
             pltpu.VMEM((rows, width), jnp.bfloat16),
             pltpu.VMEM((4, 8, rows), jnp.float32),
+            pltpu.VMEM(cache_blocks.shape, jnp.bfloat16),
+            pltpu.VMEM((2, rows, width), jnp.bfloat16),
+            pltpu.VMEM((2, 4, rows, width), jnp.bfloat16),
+            pltpu.VMEM((rows, width), jnp.bfloat16),
+            pltpu.VMEM((rows, 2 * width), jnp.float32),
+            wide,
+            pltpu.VMEM((rows, width), jnp.bfloat16),
+            dma(()), dma((width // LANES,)), dma((width // LANES,)),
             dma(()), dma(()), dma((8,)), dma((4,)), dma((4,)), dma((4,)),
             dma((4,)), dma((3,)), dma(()), dma(()),
             dma((2, 4)), dma((2,)), dma((2,)), dma((2,)), dma((2, 4)),
         ],
         compiler_params=pltpu.CompilerParams(
-            collective_id=0, has_side_effects=True, vmem_limit_bytes=60 * 2**20
+            collective_id=0, has_side_effects=True, vmem_limit_bytes=63 * 2**20
         ),
     )(
         latents, query_weight, mod_shift[None], mod_scale[None], query_gain[None],
-        keys, values, group_index,
-    )
-
-
-def attend_kernel(counts_ref, q_ref, k_ref, v_ref, o_ref):
-    span, slots = k_ref.shape[0], k_ref.shape[1]
-    factor = math.log2(math.e) / math.sqrt(HD)
-    query = q_ref[...]
-    place = lax.broadcasted_iota(jnp.int32, (1, slots), 1)
-    scores = []
-    for j in range(span):
-        raw = lax.dot_general(
-            query, k_ref[j], (((1,), (1,)), ((), ())), preferred_element_type=jnp.float32
-        )
-        scores.append(jnp.where(place < counts_ref[j], raw, -1e30))
-    top = functools.reduce(
-        jnp.maximum, [jnp.max(s, axis=1, keepdims=True) for s in scores]
-    )
-    totals = jnp.zeros_like(top)
-    mixed = jnp.zeros(o_ref.shape, jnp.float32)
-    for j in range(span):
-        weights = jnp.exp2((scores[j] - top) * factor)
-        totals += jnp.sum(weights, axis=1, keepdims=True)
-        mixed += jnp.dot(
-            weights.astype(jnp.bfloat16), v_ref[j], preferred_element_type=jnp.float32
-        )
-    o_ref[...] = (mixed / totals).astype(jnp.bfloat16)
-
-
-def attend(counts, queries, keys, values):
-    rows, width = queries.shape
-    span = keys.shape[0]
-    block = 304
-    whole = pl.BlockSpec((span, rows, HD), lambda h, i: (0, 0, h))
-    return pl.pallas_call(
-        attend_kernel,
-        grid=(width // HD, pl.cdiv(rows, block)),
-        out_shape=jax.ShapeDtypeStruct((rows, width), jnp.bfloat16),
-        in_specs=[
-            pl.BlockSpec(memory_space=pltpu.SMEM),
-            pl.BlockSpec((block, HD), lambda h, i: (i, h)),
-            whole, whole,
-        ],
-        out_specs=pl.BlockSpec((block, HD), lambda h, i: (i, h)),
-        compiler_params=pltpu.CompilerParams(vmem_limit_bytes=48 * 2**20),
-    )(counts, queries, keys, values)
-
-
-def swap_pairs():
-    pairs = []
-    for tile in range(8):
-        for head in range(4):
-            here = tile * 4 + head
-            there = here if tile % 2 == head % 2 else (tile ^ 1) * 4 + (head ^ 1)
-            pairs.append((here, there))
-    return pairs
-
-
-def per_device_square(
-    latents, query_weight, mod_shift, mod_scale, query_gain, cache_blocks, block_counts, group_index
-):
-    keys, values = cache_blocks[:, 0, :], cache_blocks[:, 1, :]
-    queries, keys_all, values_all = project(
-        latents, query_weight, mod_shift, mod_scale, query_gain, keys, values, group_index
-    )
-    counts = lax.dynamic_slice_in_dim(block_counts, lax.axis_index("tile") // 4 * 4, 4)
-    attended = attend(counts, queries, keys_all, values_all)
-    return lax.ppermute(attended, ("tile", "head"), swap_pairs())
+        cache_blocks, block_counts, group_index,
+    )
 
 
 def solution(mesh):
@@ -550,7 +572,7 @@
     out_specs = P("tile", "head")
     square = mesh.shape["tile"] == 8 and mesh.shape["head"] == 4
     return jax.shard_map(
-        per_device_square if square else per_device, mesh=mesh,
+        project if square else per_device, mesh=mesh,
         in_specs=in_specs,
         out_specs=out_specs,
         check_vma=False,

time: 219 us -> 166 us (0.76); the launches traced: 216 us -> 165 us
  Pallas kernels: 183 us -> 161 us
  waiting for transfers between devices: 15.4 us -> 0 us
  local copies, waits for them, and re-layouts: 14.7 us -> 3.63 us
    pallas_call x2 -> x1, Pallas kernels: 183 us -> 161 us  [project(): pl.pallas_call(project_kernel, out_shape=jax.ShapeDtypeStruct((rows, widt...]
    ppermute x1 -> x0, waiting for transfers between devices: 15.4 us -> none  [per_device_square(): return lax.ppermute(attended, ('tile', 'head'), swap_pairs())]
    slice x1 -> x0, local copies, waits for them, and re-layouts: 7.72 us -> none  [per_device_square(): keys, values = (cache_blocks[:, 0, :], cache_blocks[:, 1, :])]
    squeeze x1 -> x0, local copies, waits for them, and re-layouts: 3.4 us -> none  [per_device_square(): keys, values = (cache_blocks[:, 0, :], cache_blocks[:, 1, :])]
  transfers between devices with their start and end apart: 1 -> 0, of which waited for: 1 -> 0; matrix products, arithmetic and copies ran while one was open for 0% -> 0% of each run, Pallas kernels for 0% -> 0%
where the time goes in v2:
time: 166 us; the launch traced here: 165 us
  Pallas kernels  161 us (97%)
  local copies, waits for them, and re-layouts  3.63 us (2%)
    pallas_call x1, Pallas kernels, project(): pl.pallas_call(project_kernel, out_shape=jax.ShapeDtypeStruct((rows, widt...  161 us

profile of v2, /device:TPU:1, one launch (start us, length us, event | category | flops | bytes accessed | tf_op | source)
XLA Modules:
  0.0 165.4 jit_solution(10372468475982996697)
XLA Ops:
  0.7 1.3 broadcast_in_dim.11.gain_ref
  1.9 161.1 %shard_map.82 = bf16[900,640]{1,0:T(8,128)(2,1)} custom-call(bf16[900,5120]{1,0:T(8,128)(2,1)} %lat_ref.1, bf16[640,640]{1,0:T(8,128)(2,1)} %w_ref.1, f32[1,5120]{1,0:T(1,128)} %bitcast.2, f32[1,5120]{1,0:T(1,128)} %bitcast.3, f32[1,640]{1,0:T(1,128)} %broadcast_in_dim.11.gain_ref, bf16[900,2,640]{2,1,0:T(2,128)(2,1)} %cache_ref.1, s32[8]{0:T(128)} %counts_ref.1, ...), custom_call_target="tpu_custom_call" | custom-call | tf_op jit(solution)/shard_map/pallas_call | solution.py:528
  163.1 2.4 %copy.11 = bf16[900,640]{1,0:T(8,128)(2,1)} copy(bf16[900,640]{1,0:T(8,128)(2,1)} %shard_map.82) | data formatting | bytes 2304000
